TPU v7x, 128 devices: a whole 4x4x4 slice. The times are simulated.
128 devices in a mesh: ctx: 64 (over y, x, z), head: 2 (over core).
Axes of the slice: x: 4, y: 4, z: 4, core: 2. Of those that a mesh axis runs over, the one named last changes fastest.
Arguments:
- hidden: bfloat16 [16384, 4096], P('ctx', 'head'), may hold values from -6 to 6
- block_owner: int32 [128], replicated, may hold values from 0 to 63, as said below
- doc_lengths: int32 [32], replicated, may hold values from 1 to 1024, 16384 in all
- w_query: bfloat16 [4096, 2048], P(None, 'head'), may hold values from -1 to 1
- w_key: bfloat16 [4096, 512], P(None, 'head'), may hold values from -1 to 1
- value_weight: bfloat16 [4096, 512], P(None, 'head'), may hold values from -0.09375 to 0.09375
Outputs:
- attended: bfloat16 [16384, 2048], P('ctx', 'head')
Inputs may be any that keep to these rules, and one draw needn't show every extreme that they name: `block_owner`: owners never fall along the blocks; context shard j holds a run of blocks (possibly empty) that starts within 1 block of block j * 2, shard 0 at block 0; so a block's owner is its loader shard or a neighbour. Shard 1 starts exactly 1 block early and shard 2 starts late. Some shard holds exactly 4 blocks. `doc_lengths`: the lengths sum to 16384; the longest is exactly 1024.
All inputs are finite; a program needn't handle non-finite values.
Results may differ from a plain program's by a relative error of at most 0.008.
Values may be sent and summed in bfloat16 or wider, within the bound.
A program may use at most 128 MiB of HBM per device.

v0:
```python
import jax
import jax.numpy as jnp
from jax import lax
from jax.sharding import PartitionSpec as P

HEAD_SIZE_DIM = 128
BLK = 128
REACH = 2


def extended(x, sides, width):
    for axis, dim in sides:
        peers, length = (lax.axis_size(axis), x.shape[dim])
        up = [(i, (i + 1) % peers) for i in range(peers - 1)]
        down = [(j, i) for i, j in up]
        last = lax.slice_in_dim(x, length - width, length, axis=dim)
        first = lax.slice_in_dim(x, 0, width, axis=dim)
        before = lax.ppermute(last, axis, up)
        after = lax.ppermute(first, axis, down)
        x = jnp.concatenate([before, x, after], axis=dim)
    return x


def from_behind(block, axis, distance):
    devices = range(lax.axis_size(axis))
    route = [(i - distance, i) for i in devices if i - distance in devices]
    return lax.ppermute(block, axis, route)


def attend_block(
    query_row_set, query_pos, bound, keys_all, values_all, key_pos, key_live, head_group
):
    rows = query_row_set.shape[0]
    kv_heads = keys_all.shape[1]
    head_size = keys_all.shape[2]
    shaped = query_row_set.reshape(rows, kv_heads, head_group, head_size)
    scale = 1.0 / head_size**0.5
    scores = (
        jnp.einsum("qhgd,khd->hgqk", shaped, keys_all, preferred_element_type=jnp.float32) * scale
    )
    allowed = (
        (key_pos[None, :] >= bound[:, None])
        & (key_pos[None, :] <= query_pos[:, None])
        & key_live[None, :]
    )
    scores = jnp.where(allowed[None, None], scores, jnp.float32(-1e30))
    largest = jnp.max(scores, axis=-1, keepdims=True)
    expo = jnp.exp(scores - largest)
    total = jnp.sum(expo, axis=-1, keepdims=True)
    weights = expo.astype(jnp.bfloat16)
    mixed = (
        jnp.einsum("hgqk,khd->hgqd", weights, values_all, preferred_element_type=jnp.float32)
        / total
    )
    return (
        jnp.transpose(mixed, (2, 0, 1, 3))
        .reshape(rows, kv_heads * head_group * head_size)
        .astype(jnp.bfloat16)
    )


def local(hidden, block_owner, doc_lengths, w_query, w_key, value_weight):
    rows_dev = hidden.shape[0]
    per_shard = rows_dev // BLK
    half_rows = per_shard // 2 * BLK
    cap_rows = 2 * rows_dev
    query_cols = w_query.shape[1]
    key_cols = w_key.shape[1]
    head_group = query_cols // key_cols
    here = lax.axis_index("ctx")
    whole = lax.all_gather(hidden, "head", axis=1, tiled=True)

    def start_of(shard):
        return jnp.sum((block_owner < shard).astype(jnp.int32))

    begins = [start_of(here + step) for step in range(-REACH, 2)]
    offset = (begins[REACH] - here * per_shard + per_shard // 2) * BLK
    pool = extended(whole, (("ctx", 0),), half_rows)
    padded = jnp.concatenate([pool, jnp.zeros((rows_dev, pool.shape[1]), jnp.bfloat16)], axis=0)
    context = lax.dynamic_slice_in_dim(padded, offset, cap_rows, 0)
    query_matrix = jnp.dot(context, w_query, preferred_element_type=jnp.float32).astype(
        jnp.bfloat16
    )
    key_matrix = jnp.dot(context, w_key, preferred_element_type=jnp.float32).astype(jnp.bfloat16)
    value_matrix = jnp.dot(context, value_weight, preferred_element_type=jnp.float32).astype(
        jnp.bfloat16
    )
    paired = jnp.concatenate([key_matrix, value_matrix], axis=1)
    earlier = []
    current = paired
    for distance in range(REACH):
        current = from_behind(current, "ctx", 1)
        earlier.append(current)
    ordered = earlier[::-1] + [paired]
    key_set = jnp.concatenate(ordered, axis=0)
    kv_heads = key_cols // HEAD_SIZE_DIM
    keys_all = key_set[:, :key_cols].reshape(key_set.shape[0], kv_heads, HEAD_SIZE_DIM)
    values_all = key_set[:, key_cols:].reshape(key_set.shape[0], kv_heads, HEAD_SIZE_DIM)
    row_index = jnp.arange(cap_rows, dtype=jnp.int32)
    key_pos = jnp.concatenate([begins[slot] * BLK + row_index for slot in range(REACH + 1)])
    key_live = jnp.concatenate(
        [row_index < (begins[slot + 1] - begins[slot]) * BLK for slot in range(REACH + 1)]
    )
    query_pos = begins[REACH] * BLK + row_index
    query_live = row_index < (begins[REACH + 1] - begins[REACH]) * BLK
    ends = jnp.cumsum(doc_lengths)
    doc_start = jnp.sum(
        doc_lengths[None, :] * (ends[None, :] <= query_pos[:, None]).astype(jnp.int32), axis=1
    )
    query_block = min(512, cap_rows)
    count = cap_rows // query_block

    def one_block(pieces):
        return attend_block(
            pieces[0], pieces[1], pieces[2], keys_all, values_all, key_pos, key_live, head_group
        )

    outputs = lax.map(
        one_block,
        (
            query_matrix.reshape(count, query_block, query_cols),
            query_pos.reshape(count, query_block),
            doc_start.reshape(count, query_block),
        ),
    )
    outputs = outputs.reshape(cap_rows, query_cols)
    outputs = jnp.where(query_live[:, None], outputs, jnp.zeros_like(outputs))
    placed = lax.dynamic_update_slice_in_dim(
        jnp.zeros((2 * cap_rows, query_cols), jnp.bfloat16), outputs, offset, 0
    )[:cap_rows]
    result = placed[half_rows : half_rows + rows_dev]
    arrived = []
    for distance, piece in ((1, placed[half_rows + rows_dev :]), (-1, placed[:half_rows])):
        arrived.append(from_behind(piece, "ctx", distance))
    result = result.at[:half_rows].add(arrived[0])
    result = result.at[rows_dev - half_rows :].add(arrived[1])
    return result


def solution(mesh):
    in_specs = (P("ctx", "head"), P(), P(), P(None, "head"), P(None, "head"), P(None, "head"))
    out_specs = P("ctx", "head")
    return jax.shard_map(local, mesh=mesh, in_specs=in_specs, out_specs=out_specs, check_vma=False)
```

profile of v0, /device:TPU:24, one launch (start us, length us, event | category | flops | bytes accessed | tf_op | source)
XLA Modules:
  0.0 170.6 jit_solution(5032078428125998565)
XLA Ops:
  7.3 17.2 %all-gather.2.cloned.1.call-done = bf16[256,4096]{1,0:T(8,128)(2,1)} async-done(((bf16[256,2048]{1,0:T(8,128)(2,1)}), bf16[256,4096]{1,0:T(8,128)(2,1)}) %all-gather.2.cloned.1.call-update) | async-done | bytes 2097168 | tf_op jit(solution)/shard_map/all_gather | solution.py:71
  24.5 3.1 %fusion.23 = (bf16[128,4096]{1,0:T(8,128)(2,1)}, bf16[128,4096]{1,0:T(8,128)(2,1)}) fusion(bf16[256,4096]{1,0:T(8,128)(2,1)} %all-gather.2.cloned.1.call-done), kind=kLoop, calls=%fused_computation.49 | loop fusion | bytes 4194304 | tf_op jit(solution)/shard_map/slice | solution.py:17
  27.6 3.4 %collective-permute-start = (bf16[128,4096]{1,0:T(8,128)(2,1)}, bf16[128,4096]{1,0:T(8,128)(2,1)S(1)}, u32[]{:S(2)}, u32[]{:S(2)}) collective-permute-start(bf16[128,4096]{1,0:T(8,128)(2,1)} %get-tuple-element.63), channel_id=1, source_target_pairs={{0,2},{2,4},{4,6},{6,8},{8,10},{10,12},{12,14},{14,16},{16,18},{18... | collective-permute-start | bytes 3145736 | tf_op jit(solution)/shard_map/ppermute | solution.py:18
  31.1 6.6 %collective-permute-start.1 = (bf16[128,4096]{1,0:T(8,128)(2,1)}, bf16[128,4096]{1,0:T(8,128)(2,1)}, u32[]{:S(2)}, u32[]{:S(2)}) collective-permute-start(bf16[128,4096]{1,0:T(8,128)(2,1)} %get-tuple-element.62), channel_id=1, source_target_pairs={{2,0},{4,2},{6,4},{8,6},{10,8},{12,10},{14,12},{16,14},{18,16},{20... | collective-permute-start | bytes 3145736 | tf_op jit(solution)/shard_map/ppermute | solution.py:19
  45.5 13.9 %collective-permute-done = bf16[128,4096]{1,0:T(8,128)(2,1)S(1)} collective-permute-done((bf16[128,4096]{1,0:T(8,128)(2,1)}, bf16[128,4096]{1,0:T(8,128)(2,1)S(1)}, u32[]{:S(2)}, u32[]{:S(2)}) %collective-permute-start) | collective-permute-done | bytes 1048608 | tf_op jit(solution)/shard_map/ppermute | solution.py:18
  60.6 5.0 %fusion.8 = bf16[512,4096]{1,0:T(8,128)(2,1)S(1)} fusion(s32[]{:T(128)S(6)} %select_n.15, bf16[128,4096]{1,0:T(8,128)(2,1)S(1)} %collective-permute-done, bf16[256,4096]{1,0:T(8,128)(2,1)} %all-gather.2.cloned.1.call-done, bf16[128,4096]{1,0:T(8,128)(2,1)} %collective-permute-done.1, bf16[512]{0:T(512)(128)(2,1)S(1)} %pad_dynamic-slice_fusion.3), kind=kLoop, calls=%fused_computation.12 | loop fusion | flops 16777216 | bytes 8389636 | tf_op jit(solution)/shard_map/concatenate | solution.py:79
  65.6 1.3 convolution_convert_fusion.1
  68.7 1.3 convolution_convert_fusion.2
  70.9 1.9 %collective-permute-start.2 = (bf16[512,512]{0,1:T(8,128)(2,1)}, bf16[512,512]{0,1:T(8,128)(2,1)}, u32[]{:S(2)}, u32[]{:S(2)}) collective-permute-start(bf16[512,512]{0,1:T(8,128)(2,1)} %pad_maximum_fusion), channel_id=1, source_target_pairs={{0,2},{2,4},{4,6},{6,8},{8,10},{10,12},{12,14},{14,16},{16,18},{18... | collective-permute-start | bytes 1572872 | tf_op jit(solution)/shard_map/ppermute | solution.py:27
  73.9 17.2 %collective-permute-done.2 = bf16[512,512]{0,1:T(8,128)(2,1)} collective-permute-done((bf16[512,512]{0,1:T(8,128)(2,1)}, bf16[512,512]{0,1:T(8,128)(2,1)}, u32[]{:S(2)}, u32[]{:S(2)}) %collective-permute-start.2) | collective-permute-done | bytes 524320 | tf_op jit(solution)/shard_map/ppermute | solution.py:27
  91.2 2.1 %collective-permute-start.3 = (bf16[512,512]{0,1:T(8,128)(2,1)}, bf16[512,512]{0,1:T(8,128)(2,1)}, u32[]{:S(2)}, u32[]{:S(2)}) collective-permute-start(bf16[512,512]{0,1:T(8,128)(2,1)} %collective-permute-done.2), channel_id=1, source_target_pairs={{0,2},{2,4},{4,6},{6,8},{8,10},{10,12},{12,14},{14,16},{16,18},{18... | collective-permute-start | bytes 1572872 | tf_op jit(solution)/shard_map/ppermute | solution.py:27
  93.3 10.1 %convolution_convert_fusion = bf16[512,1024]{1,0:T(8,128)(2,1)} fusion(bf16[512,4096]{1,0:T(8,128)(2,1)} %copy-done.1, bf16[4096,1024]{1,0:T(8,128)(2,1)} %param.13), kind=kOutput, calls=%fused_computation.17 | convolution fusion | flops 4295491584 | bytes 13631488 | tf_op jit(solution)/shard_map/dot_general | solution.py:81
  103.4 2.6 %reshape.184 = bf16[512,2,4,128]{3,2,1,0:T(4,128)(2,1)} reshape(bf16[512,1024]{1,0:T(8,128)(2,1)} %convolution_convert_fusion) | data formatting | bytes 2097152 | tf_op jit(solution)/shard_map/while/body/eval_jaxpr/reshape | solution.py:36
  106.0 4.0 %collective-permute-done.3 = bf16[512,512]{0,1:T(8,128)(2,1)} collective-permute-done((bf16[512,512]{0,1:T(8,128)(2,1)}, bf16[512,512]{0,1:T(8,128)(2,1)}, u32[]{:S(2)}, u32[]{:S(2)}) %collective-permute-start.3) | collective-permute-done | bytes 524320 | tf_op jit(solution)/shard_map/ppermute | solution.py:27
  110.0 1.3 maximum_maximum_fusion
  111.4 10.6 %fusion.2 = (f32[2,4,512]{2,1,0:T(4,128)S(1)}, f32[2,1536,512,4]{2,1,3,0:T(8,128)}) fusion(pred[512,1536]{0,1:T(8,128)(4,1)S(1)} %and_and_fusion, bf16[1536,2,128,1]{0,2,3,1:T(8,128)(2,1)S(1)} %bitcast.38, bf16[512,2,4,128]{3,2,1,0:T(4,128)(2,1)S(1)} %copy-done.3), kind=kOutput, calls=%fused_computation.4 | convolution fusion | flops 1629483008 | bytes 27803648 | tf_op jit(solution)/shard_map/while/body/eval_jaxpr/qhgd,khd->hgqk/dot_general | solution.py:39
  122.0 11.1 %fusion = f32[2,4,512]{2,1,0:T(4,128)S(1)} fusion(f32[2,1536,512,4]{2,1,3,0:T(8,128)} %get-tuple-element.67, f32[2,4,512]{2,1,0:T(4,128)S(1)} %get-tuple-element.66, pred[512,1536]{0,1:T(8,128)(4,1)S(1)} %and_and_fusion), kind=kLoop, calls=%fused_computation.2 | loop fusion | flops 25161728 | bytes 25985024 | tf_op jit(solution)/shard_map/while/body/eval_jaxpr/reduce_sum | solution.py:49
  133.1 12.9 %fusion.9 = bf16[512,2,4,128]{0,3,2,1:T(8,128)(2,1)} fusion(bf16[1536,2,128,1]{0,2,3,1:T(8,128)(2,1)S(1)} %bitcast.37, f32[2,1536,512,4]{2,1,3,0:T(8,128)} %get-tuple-element.67, f32[2,4,512]{2,1,0:T(4,128)S(1)} %get-tuple-element.66, pred[512,1536]{0,1:T(8,128)(4,1)S(1)} %and_and_fusion, f32[512,2,4]{0,2,1:T(4,128)S(1)} %bitcast.39), kind=kOutput, calls=%fused_computation.15 | convolution fusion | flops 1636827136 | bytes 27820032 | tf_op jit(solution)/shard_map/while/body/eval_jaxpr/hgqk,khd->hgqd/dot_general | solution.py:52
  146.0 1.5 copy.21
  148.1 1.9 %collective-permute-start.4 = (bf16[128,1024]{1,0:T(8,128)(2,1)S(1)}, bf16[128,1024]{1,0:T(8,128)(2,1)S(1)}, u32[]{:S(2)}, u32[]{:S(2)}) collective-permute-start(bf16[128,1024]{1,0:T(8,128)(2,1)S(1)} %get-tuple-element.61), channel_id=1, source_target_pairs={{0,2},{2,4},{4,6},{6,8},{8,10},{10,12},{12,14},{14,16},{16,18},{18... | collective-permute-start | bytes 786440 | tf_op jit(solution)/shard_map/ppermute | solution.py:27
  150.0 8.1 %collective-permute-start.5 = (bf16[128,1024]{1,0:T(8,128)(2,1)S(1)}, bf16[128,1024]{1,0:T(8,128)(2,1)S(1)}, u32[]{:S(2)}, u32[]{:S(2)}) collective-permute-start(bf16[128,1024]{1,0:T(8,128)(2,1)S(1)} %get-tuple-element.60), channel_id=1, source_target_pairs={{2,0},{4,2},{6,4},{8,6},{10,8},{12,10},{14,12},{16,14},{18,16},{20... | collective-permute-start | bytes 786440 | tf_op jit(solution)/shard_map/ppermute | solution.py:27
  158.2 2.4 %collective-permute-done.4 = bf16[128,1024]{1,0:T(8,128)(2,1)S(1)} collective-permute-done((bf16[128,1024]{1,0:T(8,128)(2,1)S(1)}, bf16[128,1024]{1,0:T(8,128)(2,1)S(1)}, u32[]{:S(2)}, u32[]{:S(2)}) %collective-permute-start.4) | collective-permute-done | bytes 262176 | tf_op jit(solution)/shard_map/ppermute | solution.py:27
  160.7 1.4 collective-permute-done.5
  162.0 1.7 %fusion.14 = bf16[256,1024]{1,0:T(8,128)(2,1)} fusion(bf16[256,1024]{1,0:T(8,128)(2,1)} %copy-done.2, bf16[128,1024]{1,0:T(8,128)(2,1)S(1)} %collective-permute-done.5), kind=kLoop, calls=%fused_computation.25 | loop fusion | flops 524288 | bytes 786432 | tf_op jit(solution)/shard_map/scatter-add | solution.py:136
  (38 shorter events, 7.7 us)
Async XLA Ops:
  6.5 59.0 %copy-start = (bf16[4096,256]{1,0:T(8,128)(2,1)S(1)}, bf16[4096,256]{1,0:T(8,128)(2,1)}, u32[]{:S(2)}) copy-start(bf16[4096,256]{1,0:T(8,128)(2,1)} %param.15) | copy-start | bytes 6291460
  6.5 31.2 %copy-start.5 = (s32[128]{0:T(128)S(1)}, s32[128]{0:T(128)}, u32[]{:S(2)}) copy-start(s32[128]{0:T(128)} %param.11) | copy-start | bytes 1540
  6.5 38.4 %copy-start.4 = (s32[32]{0:T(128)S(1)}, s32[32]{0:T(128)}, u32[]{:S(2)}) copy-start(s32[32]{0:T(128)} %param.12) | copy-start | bytes 388
  6.5 18.0 %all-gather.2.cloned.1.call-start = ((), (), s32[]{:S(2)}) async-start(), calls=%async_computation | async-start | bytes 3145728 | tf_op jit(solution)/shard_map/all_gather | solution.py:71
  27.6 31.7 %collective-permute-start = (bf16[128,4096]{1,0:T(8,128)(2,1)}, bf16[128,4096]{1,0:T(8,128)(2,1)S(1)}, u32[]{:S(2)}, u32[]{:S(2)}) collective-permute-start(bf16[128,4096]{1,0:T(8,128)(2,1)} %get-tuple-element.63), channel_id=1, source_target_pairs={{0,2},{2,4},{4,6},{6,8},{8,10},{10,12},{12,14},{14,16},{16,18},{18... | collective-permute-start | bytes 3145736 | tf_op jit(solution)/shard_map/ppermute | solution.py:18
  31.1 29.5 %collective-permute-start.1 = (bf16[128,4096]{1,0:T(8,128)(2,1)}, bf16[128,4096]{1,0:T(8,128)(2,1)}, u32[]{:S(2)}, u32[]{:S(2)}) collective-permute-start(bf16[128,4096]{1,0:T(8,128)(2,1)} %get-tuple-element.62), channel_id=1, source_target_pairs={{2,0},{4,2},{6,4},{8,6},{10,8},{12,10},{14,12},{16,14},{18,16},{20... | collective-permute-start | bytes 3145736 | tf_op jit(solution)/shard_map/ppermute | solution.py:19
  65.6 2.1 %copy-start.1 = (bf16[512,4096]{1,0:T(8,128)(2,1)}, bf16[512,4096]{1,0:T(8,128)(2,1)S(1)}, u32[]{:S(2)}) copy-start(bf16[512,4096]{1,0:T(8,128)(2,1)S(1)} %fusion.8) | copy-start | bytes 12582916
  65.6 3.1 %copy-start.6 = (bf16[4096,256]{1,0:T(8,128)(2,1)S(1)}, bf16[4096,256]{1,0:T(8,128)(2,1)}, u32[]{:S(2)}) copy-start(bf16[4096,256]{1,0:T(8,128)(2,1)} %param.14) | copy-start | bytes 6291460
  70.9 20.3 %collective-permute-start.2 = (bf16[512,512]{0,1:T(8,128)(2,1)}, bf16[512,512]{0,1:T(8,128)(2,1)}, u32[]{:S(2)}, u32[]{:S(2)}) collective-permute-start(bf16[512,512]{0,1:T(8,128)(2,1)} %pad_maximum_fusion), channel_id=1, source_target_pairs={{0,2},{2,4},{4,6},{6,8},{8,10},{10,12},{12,14},{14,16},{16,18},{18... | collective-permute-start | bytes 1572872 | tf_op jit(solution)/shard_map/ppermute | solution.py:27
  91.2 18.8 %collective-permute-start.3 = (bf16[512,512]{0,1:T(8,128)(2,1)}, bf16[512,512]{0,1:T(8,128)(2,1)}, u32[]{:S(2)}, u32[]{:S(2)}) collective-permute-start(bf16[512,512]{0,1:T(8,128)(2,1)} %collective-permute-done.2), channel_id=1, source_target_pairs={{0,2},{2,4},{4,6},{6,8},{8,10},{10,12},{12,14},{14,16},{16,18},{18... | collective-permute-start | bytes 1572872 | tf_op jit(solution)/shard_map/ppermute | solution.py:27
  106.0 5.4 %copy-start.3 = (bf16[512,2,4,128]{3,2,1,0:T(4,128)(2,1)S(1)}, bf16[512,2,4,128]{3,2,1,0:T(4,128)(2,1)}, u32[]{:S(2)}) copy-start(bf16[512,2,4,128]{3,2,1,0:T(4,128)(2,1)} %reshape.184) | copy-start | bytes 3145732
  148.1 12.5 %collective-permute-start.4 = (bf16[128,1024]{1,0:T(8,128)(2,1)S(1)}, bf16[128,1024]{1,0:T(8,128)(2,1)S(1)}, u32[]{:S(2)}, u32[]{:S(2)}) collective-permute-start(bf16[128,1024]{1,0:T(8,128)(2,1)S(1)} %get-tuple-element.61), channel_id=1, source_target_pairs={{0,2},{2,4},{4,6},{6,8},{8,10},{10,12},{12,14},{14,16},{16,18},{18... | collective-permute-start | bytes 786440 | tf_op jit(solution)/shard_map/ppermute | solution.py:27
  150.0 12.0 %collective-permute-start.5 = (bf16[128,1024]{1,0:T(8,128)(2,1)S(1)}, bf16[128,1024]{1,0:T(8,128)(2,1)S(1)}, u32[]{:S(2)}, u32[]{:S(2)}) collective-permute-start(bf16[128,1024]{1,0:T(8,128)(2,1)S(1)} %get-tuple-element.60), channel_id=1, source_target_pairs={{2,0},{4,2},{6,4},{8,6},{10,8},{12,10},{14,12},{16,14},{18,16},{20... | collective-permute-start | bytes 786440 | tf_op jit(solution)/shard_map/ppermute | solution.py:27
  160.6 1.4 copy-start.2
Sparse Core Ops, SparseCore 0:
  9.0 15.4 all-gather.1
where the time goes:
time: 172 us; the launch traced here: 171 us
  waiting for transfers between devices  58 us (34%)
  matrix products  36.3 us (21%)
  starting transfers between devices  24.1 us (14%)
  other arithmetic  22.4 us (13%)
  between operations  20.1 us (12%)
  local copies, waits for them, and re-layouts  9.61 us (6%)
    ppermute x4, waiting for transfers between devices, from_behind(): return lax.ppermute(block, axis, route)  24.9 us
    all_gather x1, waiting for transfers between devices, local(): whole = lax.all_gather(hidden, 'head', axis=1, tiled=True)  17.2 us
    ppermute x4, starting transfers between devices, from_behind(): return lax.ppermute(block, axis, route)  14.1 us
    ppermute x1, waiting for transfers between devices, extended(): before = lax.ppermute(last, axis, up)  13.9 us
    dot_general x1, matrix products, attend_block(): jnp.einsum('hgqk,khd->hgqd', weights, values_all, preferred_element_type=...  12.9 us
    reduce_sum x1, other arithmetic, attend_block(): total = jnp.sum(expo, axis=-1, keepdims=True)  11.1 us
    dot_general x1, matrix products, attend_block(): jnp.einsum('qhgd,khd->hgqk', shaped, keys_all, preferred_element_type=jnp...  10.6 us
    dot_general x1, matrix products, local(): jnp.dot(context, w_query, preferred_element_type=jnp.float32)  10.1 us
  transfers between devices with their start and end apart: 7, of which 7 were waited for; matrix products, arithmetic and copies ran while one was open for 9% of the time, Pallas kernels for 0%

commit v1 on v0

v1 whole, which is shorter than its diff:
```python
import functools
import math

import jax
import jax.numpy as jnp
from jax import lax
from jax.experimental import pallas as pl
from jax.experimental.pallas import tpu as pltpu
from jax.sharding import PartitionSpec as P

HEAD = 128
BLK = 128
REACH = 2
NEG = -1e30
MESH = pl.DeviceIdType.MESH
OWN, BACK1, BACK3, BACK2, BACK4, PASS_UP, PASS_DOWN, PASS_ROW = range(8)
NT = (((1,), (1,)), ((), ()))


def kernel(
    shards,
    hid,
    owner,
    lengths,
    w_q,
    w_k,
    w_v,
    out,
    h_own,
    h_oth,
    wq,
    wk,
    wv,
    kv_sum,
    q_sum,
    qs,
    kv,
    low_row,
    pos_row,
    m_s,
    l_s,
    acc_s,
    load_sem,
    hid_send,
    hid_recv,
    send_sem,
    recv_sem,
):
    here = lax.axis_index("ctx")
    head = lax.axis_index("head")
    z = lax.rem(here, 4)
    ring = here - z
    up = ring + lax.rem(z + 1, 4)
    down = ring + lax.rem(z + 3, 4)
    row_next = lax.rem(here + 4, shards)
    row_prev = lax.rem(here + shards - 4, shards)
    half = h_own.shape[1]
    mine = pl.multiple_of(head * half, half)
    other = pl.multiple_of((1 - head) * half, half)

    loads = [pltpu.make_async_copy(hid, h_own, load_sem.at[0])]
    for part, first in ((0, mine), (1, other)):
        for src, dst in ((w_k, wk), (w_v, wv)):
            loads.append(
                pltpu.make_async_copy(
                    src.at[pl.ds(first, half)], dst.at[part], load_sem.at[len(loads)]
                )
            )
    for part, first in ((0, mine), (1, other)):
        loads.append(
            pltpu.make_async_copy(
                w_q.at[pl.ds(first, half)], wq.at[part], load_sem.at[len(loads)]
            )
        )
    for load in loads:
        load.start()
    load_h, load_k0, load_v0, load_k1, load_v1, load_q0, load_q1 = loads

    barrier = pltpu.get_barrier_semaphore()
    for peer in ((here, 1 - head), (up, head), (down, head), (row_prev, head)):
        pl.semaphore_signal(barrier, inc=1, device_id=peer, device_id_type=MESH)
    pl.semaphore_wait(barrier, 4)

    swaps = []
    for blk in range(2):
        rows = pl.ds(blk * BLK, BLK)
        swaps.append(
            pltpu.make_async_remote_copy(
                src_ref=hid.at[rows],
                dst_ref=h_oth.at[rows],
                send_sem=hid_send.at[blk],
                recv_sem=hid_recv.at[blk],
                device_id=(here, 1 - head),
                device_id_type=MESH,
            )
        )
        swaps[-1].start()

    first_block = 2 * here - 8
    lane = lax.broadcasted_iota(jnp.int32, (8, BLK), 1)
    for blk in range(2):
        shard = owner[2 * here + blk]
        low = jnp.maximum(first_block, 0)
        for j in range(10):
            block = first_block + j
            below = owner[jnp.maximum(block, 0)] < shard - REACH
            low = low + jnp.where(below & (block >= 0), 1, 0)
        pos = (2 * here + blk) * BLK + lane
        start = jnp.int32(0)
        doc = jnp.zeros((8, BLK), jnp.int32)
        for i in range(lengths.shape[0]):
            doc = jnp.where(pos >= start, start, doc)
            start = start + lengths[i]
        lower = jnp.maximum(doc, low * BLK)
        for hh in range(4):
            cols = slice((blk * 4 + hh) * BLK, (blk * 4 + hh + 1) * BLK)
            low_row[:, cols] = lower
            pos_row[:, cols] = pos

    def copy(src, dst, piece, to, k):
        return pltpu.make_async_remote_copy(
            src_ref=kv.at[src, piece],
            dst_ref=kv.at[dst, piece],
            send_sem=send_sem.at[k],
            recv_sem=recv_sem.at[dst, piece],
            device_id=(to, head),
            device_id_type=MESH,
        )

    sends = [0, 0, 0, 0]
    waited = [set(), set(), set(), set()]

    def send(col, src, dst, piece, to):
        copy(src, dst, piece, to, sends[col]).start()
        sends[col] += 1

    def arrive(col, slot, piece):
        if (slot, piece) not in waited[col]:
            waited[col].add((slot, piece))
            copy(OWN, slot, piece, up, 0).wait_recv()

    def by_column(step):
        for col in range(4):
            pl.when(z == col)(functools.partial(step, col))

    A, B = (0, 1), (2, 3)

    def send_first(col):
        for a in A:
            send(col, OWN, BACK1 if col < 3 else PASS_UP, a, up)
            send(col, OWN, PASS_DOWN if col > 0 else BACK3, a, down)

    def send_second(col):
        for b in B:
            send(col, OWN, BACK4, b, row_next)
            if col < 3:
                send(col, OWN, BACK1, b, up)
            if col == 0:
                send(col, OWN, BACK3, b, down)

    def relay_first(i, col):
        a, b = A[i], B[i]
        if col == 0:
            arrive(col, PASS_DOWN, a)
            send(col, PASS_DOWN, BACK3, a, row_next)
            send(col, PASS_DOWN, BACK2, a, down)
            arrive(col, PASS_UP, a)
            send(col, PASS_UP, BACK1, a, row_next)
        if col in (1, 2):
            arrive(col, PASS_DOWN, a)
            send(col, PASS_DOWN, BACK3, a, row_next)
        if col == 1:
            arrive(col, BACK1, a)
            send(col, BACK1, BACK2, a, up)
        if col == 3:
            arrive(col, BACK1, a)
            send(col, BACK1, PASS_ROW, a, row_next)
        if col > 0:
            arrive(col, BACK4, b)
            send(col, BACK4, BACK3, b, down)
        if col == 3:
            send(col, BACK4, BACK1, b, up)

    def relay_second(i, col):
        b = B[i]
        if col == 2:
            arrive(col, BACK1, b)
            send(col, BACK1, BACK2, b, up)
        if col == 3:
            arrive(col, BACK3, b)
            send(col, BACK3, BACK2, b, down)

    def relay_third(i, col):
        a, b = A[i], B[i]
        if col == 0:
            arrive(col, BACK1, b)
            send(col, BACK1, BACK2, b, up)
        if col == 1:
            arrive(col, BACK3, b)
            send(col, BACK3, BACK2, b, down)
        if col == 2:
            arrive(col, BACK3, a)
            send(col, BACK3, BACK2, a, down)
        if col == 3:
            arrive(col, PASS_ROW, a)
            send(col, PASS_ROW, BACK2, a, up)

    def all_of(slots_pieces):
        def step(col):
            for slot, piece in slots_pieces:
                arrive(col, slot, piece)

        by_column(step)

    def mm(x, w):
        return jnp.dot(x, w, preferred_element_type=jnp.float32)

    load_h.wait()
    load_k0.wait()
    kv_sum[:, 0:256] = mm(h_own[...], wk[0])
    load_v0.wait()
    kv_sum[:, 256:512] = mm(h_own[...], wv[0])
    load_q0.wait()

    def q_own(n, _):
        cols = pl.ds(pl.multiple_of(n * 256, 256), 256)
        q_sum[:, cols] = mm(h_own[...], wq[0, :, cols])
        return 0

    lax.fori_loop(0, 4, q_own, 0)

    for blk in range(2):
        swaps[blk].wait_recv()
        if blk == 0:
            load_k1.wait()
            load_v1.wait()
        rows = slice(blk * BLK, (blk + 1) * BLK)
        keys = kv_sum[rows, 0:256] + mm(h_oth[rows], wk[1])
        values = kv_sum[rows, 256:512] + mm(h_oth[rows], wv[1])
        for g in range(2):
            cols = slice(g * HEAD, (g + 1) * HEAD)
            kv[OWN, 2 * blk + g, 0:128] = keys[:, cols].astype(jnp.bfloat16)
            kv[OWN, 2 * blk + g, 128:256] = values[:, cols].T.astype(jnp.bfloat16)
        by_column(send_first if blk == 0 else send_second)

    load_q1.wait()

    def q_oth(n, _):
        cols = pl.ds(pl.multiple_of(n * 256, 256), 256)
        q = (q_sum[:, cols] + mm(h_oth[...], wq[1, :, cols])).astype(jnp.bfloat16)
        g, pair = n // 2, lax.rem(n, 2)
        for blk in range(2):
            for j in range(2):
                first = pl.multiple_of((blk * 4 + pair * 2 + j) * BLK, BLK)
                qs[g, pl.ds(first, BLK)] = q[blk * BLK : (blk + 1) * BLK, j * HEAD : (j + 1) * HEAD]
        return 0

    lax.fori_loop(0, 4, q_oth, 0)

    factor = math.log2(math.e) / math.sqrt(HEAD)

    def update(g, chunk, blocks, causal=False, first=False, last=False):
        lanes = pl.ds(pl.multiple_of(chunk * 256, 256), 256)
        q = qs[g, lanes]
        low = low_row[0:1, lanes]
        scores = []
        for slot, blk, back in blocks:
            s = lax.dot_general(
                kv[slot, 2 * blk + g, 0:128], q, NT, preferred_element_type=jnp.float32
            )
            k_pos = ((here - back) * 2 + blk) * BLK + lax.broadcasted_iota(
                jnp.int32, (BLK, 256), 0
            )
            allowed = k_pos >= low
            if causal:
                allowed = allowed & (k_pos <= pos_row[0:1, lanes])
            scores.append(jnp.where(allowed, s * factor, NEG))
        top = functools.reduce(jnp.maximum, [jnp.max(s, axis=0, keepdims=True) for s in scores])
        if not first:
            old = m_s[g, 0:1, lanes]
            top = jnp.maximum(old, top)
            shrink = jnp.exp2(old - top)
        parts = [jnp.exp2(s - top) for s in scores]
        total = sum(jnp.sum(p.reshape(BLK // 8, 8, 256), axis=0) for p in parts)
        weights = jnp.concatenate([p.astype(jnp.bfloat16) for p in parts], axis=0)
        values = jnp.concatenate([kv[slot, 2 * blk + g, 128:256] for slot, blk, _ in blocks], axis=1)
        mixed = mm(values, weights)
        if not first:
            total = total + l_s[g, :, lanes] * shrink
            mixed = mixed + acc_s[g, :, lanes] * shrink
        if not last:
            m_s[g, 0:1, lanes] = top
            l_s[g, :, lanes] = total
            acc_s[g, :, lanes] = mixed
            return
        mixed = mixed / jnp.sum(total, axis=0, keepdims=True)
        blk, pair = chunk // 2, lax.rem(chunk, 2)
        rows = pl.ds(pl.multiple_of(blk * BLK, BLK), BLK)
        for j in range(2):
            cols = pl.ds(pl.multiple_of((g * 4 + pair * 2 + j) * HEAD, HEAD), HEAD)
            out[rows, cols] = mixed[:, j * HEAD : (j + 1) * HEAD].T.astype(jnp.bfloat16)

    def sweep(g, chunks, blocks, **how):
        def step(chunk, _):
            update(g, chunk, blocks, **how)
            return 0

        lax.fori_loop(chunks[0], chunks[1], step, 0)

    for g in range(2):
        sweep(g, (0, 2), [(OWN, 0, 0)], causal=True, first=True)
        sweep(g, (2, 4), [(OWN, 0, 0), (OWN, 1, 0)], causal=True, first=True)

    for step in (relay_first, relay_second, relay_third):
        for i in range(2):
            by_column(functools.partial(step, i))

    for g in range(2):
        all_of([(BACK1, g), (BACK1, 2 + g)])
        sweep(g, (0, 4), [(BACK1, 0, 1), (BACK1, 1, 1)])
    for g in range(2):
        all_of([(BACK3, g), (BACK3, 2 + g), (BACK4, 2 + g)])
        sweep(g, (0, 2), [(BACK4, 1, 4), (BACK3, 0, 3), (BACK3, 1, 3)])
        sweep(g, (2, 4), [(BACK3, 1, 3)])
    for g in range(2):
        all_of([(BACK2, g), (BACK2, 2 + g)])
        sweep(g, (0, 4), [(BACK2, 0, 2), (BACK2, 1, 2)], last=True)

    for swap in swaps:
        swap.wait_send()

    def finish(col):
        for k in range(sends[col]):
            copy(OWN, BACK1, 0, up, k).wait_send()

    by_column(finish)


def local(hidden, block_owner, doc_lengths, w_query, w_key, value_weight):
    rows, half = hidden.shape
    q_cols, k_cols = w_query.shape[1], w_key.shape[1]
    groups = k_cols // HEAD
    shards = lax.axis_size("ctx")
    bf16, f32 = jnp.bfloat16, jnp.float32
    lanes = rows * q_cols // k_cols
    dma = pltpu.SemaphoreType.DMA
    any_spec = pl.BlockSpec(memory_space=pl.ANY)
    smem_spec = pl.BlockSpec(memory_space=pltpu.SMEM)
    macs = rows * 2 * half * (q_cols + 2 * k_cols)
    return pl.pallas_call(
        functools.partial(kernel, shards),
        out_shape=jax.ShapeDtypeStruct((rows, q_cols), bf16),
        in_specs=[any_spec, smem_spec, smem_spec, any_spec, any_spec, any_spec],
        out_specs=pl.BlockSpec(memory_space=pltpu.VMEM),
        scratch_shapes=[
            pltpu.VMEM((rows, half), bf16),
            pltpu.VMEM((rows, half), bf16),
            pltpu.VMEM((2, half, q_cols), bf16),
            pltpu.VMEM((2, half, k_cols), bf16),
            pltpu.VMEM((2, half, k_cols), bf16),
            pltpu.VMEM((rows, 2 * k_cols), f32),
            pltpu.VMEM((rows, q_cols), f32),
            pltpu.VMEM((groups, lanes, HEAD), bf16),
            pltpu.VMEM((8, 4, 2 * BLK, HEAD), bf16),
            pltpu.VMEM((8, lanes), jnp.int32),
            pltpu.VMEM((8, lanes), jnp.int32),
            pltpu.VMEM((groups, 8, lanes), f32),
            pltpu.VMEM((groups, 8, lanes), f32),
            pltpu.VMEM((groups, HEAD, lanes), f32),
            dma((7,)),
            dma((2,)),
            dma((2,)),
            dma((20,)),
            dma((8, 4)),
        ],
        compiler_params=pltpu.CompilerParams(
            collective_id=0, has_side_effects=True, vmem_limit_bytes=56 << 20
        ),
        cost_estimate=pl.CostEstimate(
            flops=4 * macs, bytes_accessed=16 << 20, transcendentals=2 << 20
        ),
        name="attention",
    )(hidden, block_owner, doc_lengths, w_query, w_key, value_weight)


def solution(mesh):
    in_specs = (P("ctx", "head"), P(), P(), P(None, "head"), P(None, "head"), P(None, "head"))
    out_specs = P("ctx", "head")
    return jax.shard_map(local, mesh=mesh, in_specs=in_specs, out_specs=out_specs, check_vma=False)
```

time: 172 us -> 37.9 us (0.22)
  the two profiles are of different devices: /device:TPU:24 before, /device:TPU:0 now
where the time goes in v1:
time: 37.9 us; the launch traced here: 37.8 us
  Pallas kernels  35.9 us (95%)
  local copies, waits for them, and re-layouts  1.87 us (5%)
    pallas_call x1, Pallas kernels, local(): pl.pallas_call(functools.partial(kernel, shards), out_shape=jax.ShapeDtyp...  35.9 us
    unnamed x1, local copies, waits for them, and re-layouts  1.87 us

profile of v1, /device:TPU:0, one launch (start us, length us, event | category | flops | bytes accessed | tf_op | source)
XLA Modules:
  0.0 37.8 jit_solution(13945547105184699610)
XLA Ops:
  0.0 35.9 %attention.1 = bf16[256,1024]{1,0:T(8,128)(2,1)} custom-call(bf16[256,2048]{1,0:T(8,128)(2,1)} %hid.1, s32[128]{0:T(128)} %owner.1, s32[32]{0:T(128)} %lengths.1, bf16[4096,1024]{1,0:T(8,128)(2,1)} %w_q.1, bf16[4096,256]{1,0:T(8,128)(2,1)} %w_k.1, bf16[4096,256]{1,0:T(8,128)(2,1)} %w_v.1), custom_call_target="tpu_custom_call" | custom-call | flops 6442450944 | bytes 16777216 | tf_op jit(solution)/shard_map/attention/pallas_call | solution.py:350
  35.9 1.9 %copy.8 = bf16[256,1024]{1,0:T(8,128)(2,1)} copy(bf16[256,1024]{1,0:T(8,128)(2,1)} %attention.1) | data formatting | bytes 1048576

commit v2 on v1

--- a/solution.py
+++ b/solution.py
@@ -14,7 +14,6 @@
 NEG = -1e30
 MESH = pl.DeviceIdType.MESH
 OWN, BACK1, BACK3, BACK2, BACK4, PASS_UP, PASS_DOWN, PASS_ROW = range(8)
-NT = (((1,), (1,)), ((), ()))
 
 
 def kernel(
@@ -40,6 +39,9 @@
     m_s,
     l_s,
     acc_s,
+    s_buf,
+    p_buf,
+    shrink_s,
     load_sem,
     hid_send,
     hid_recv,
@@ -75,6 +77,11 @@
     for load in loads:
         load.start()
     load_h, load_k0, load_v0, load_k1, load_v1, load_q0, load_q1 = loads
+
+    @pl.when(here < 4)
+    def _():
+        for slot in (BACK1, BACK3, BACK2, BACK4):
+            kv[slot] = jnp.zeros(kv.shape[1:], kv.dtype)
 
     barrier = pltpu.get_barrier_semaphore()
     for peer in ((here, 1 - head), (up, head), (down, head), (row_prev, head)):
@@ -127,17 +134,38 @@
             device_id_type=MESH,
         )
 
-    sends = [0, 0, 0, 0]
+    first_row, last_row = here < 4, here >= shards - 4
+    sends = [[0] * 3 for _ in range(4)]
     waited = [set(), set(), set(), set()]
 
-    def send(col, src, dst, piece, to):
-        copy(src, dst, piece, to, sends[col]).start()
-        sends[col] += 1
+    ALWAYS, CROSS, LATER = range(3)
+
+    def guarded(kind, action):
+        if kind == ALWAYS:
+            action()
+        else:
+            pl.when(jnp.logical_not(last_row if kind == CROSS else first_row))(action)
+
+    def send(col, src, dst, piece, to, kind=ALWAYS):
+        k = 8 * kind + sends[col][kind]
+        sends[col][kind] += 1
+        guarded(kind, lambda: copy(src, dst, piece, to, k).start())
+
+    def from_row_before(col, slot):
+        return (
+            slot in (BACK4, PASS_ROW)
+            or (slot == BACK1 and col == 0)
+            or (slot == BACK3 and col < 3)
+            or (slot == BACK2 and col < 2)
+        )
 
     def arrive(col, slot, piece):
         if (slot, piece) not in waited[col]:
             waited[col].add((slot, piece))
-            copy(OWN, slot, piece, up, 0).wait_recv()
+            guarded(
+                LATER if from_row_before(col, slot) else ALWAYS,
+                lambda: copy(OWN, slot, piece, up, 0).wait_recv(),
+            )
 
     def by_column(step):
         for col in range(4):
@@ -152,7 +180,7 @@
 
     def send_second(col):
         for b in B:
-            send(col, OWN, BACK4, b, row_next)
+            send(col, OWN, BACK4, b, row_next, CROSS)
             if col < 3:
                 send(col, OWN, BACK1, b, up)
             if col == 0:
@@ -162,24 +190,24 @@
         a, b = A[i], B[i]
         if col == 0:
             arrive(col, PASS_DOWN, a)
-            send(col, PASS_DOWN, BACK3, a, row_next)
+            send(col, PASS_DOWN, BACK3, a, row_next, CROSS)
             send(col, PASS_DOWN, BACK2, a, down)
             arrive(col, PASS_UP, a)
-            send(col, PASS_UP, BACK1, a, row_next)
+            send(col, PASS_UP, BACK1, a, row_next, CROSS)
         if col in (1, 2):
             arrive(col, PASS_DOWN, a)
-            send(col, PASS_DOWN, BACK3, a, row_next)
+            send(col, PASS_DOWN, BACK3, a, row_next, CROSS)
         if col == 1:
             arrive(col, BACK1, a)
             send(col, BACK1, BACK2, a, up)
         if col == 3:
             arrive(col, BACK1, a)
-            send(col, BACK1, PASS_ROW, a, row_next)
+            send(col, BACK1, PASS_ROW, a, row_next, CROSS)
         if col > 0:
             arrive(col, BACK4, b)
-            send(col, BACK4, BACK3, b, down)
+            send(col, BACK4, BACK3, b, down, LATER)
         if col == 3:
-            send(col, BACK4, BACK1, b, up)
+            send(col, BACK4, BACK1, b, up, LATER)
 
     def relay_second(i, col):
         b = B[i]
@@ -194,16 +222,16 @@
         a, b = A[i], B[i]
         if col == 0:
             arrive(col, BACK1, b)
-            send(col, BACK1, BACK2, b, up)
+            send(col, BACK1, BACK2, b, up, LATER)
         if col == 1:
             arrive(col, BACK3, b)
-            send(col, BACK3, BACK2, b, down)
+            send(col, BACK3, BACK2, b, down, LATER)
         if col == 2:
             arrive(col, BACK3, a)
-            send(col, BACK3, BACK2, a, down)
+            send(col, BACK3, BACK2, a, down, LATER)
         if col == 3:
             arrive(col, PASS_ROW, a)
-            send(col, PASS_ROW, BACK2, a, up)
+            send(col, PASS_ROW, BACK2, a, up, LATER)
 
     def all_of(slots_pieces):
         def step(col):
@@ -252,86 +280,105 @@
         for blk in range(2):
             for j in range(2):
                 first = pl.multiple_of((blk * 4 + pair * 2 + j) * BLK, BLK)
-                qs[g, pl.ds(first, BLK)] = q[blk * BLK : (blk + 1) * BLK, j * HEAD : (j + 1) * HEAD]
+                qs[g, :, pl.ds(first, BLK)] = q[blk * BLK : (blk + 1) * BLK, j * HEAD : (j + 1) * HEAD].T
         return 0
 
     lax.fori_loop(0, 4, q_oth, 0)
 
     factor = math.log2(math.e) / math.sqrt(HEAD)
 
-    def update(g, chunk, blocks, causal=False, first=False, last=False):
-        lanes = pl.ds(pl.multiple_of(chunk * 256, 256), 256)
-        q = qs[g, lanes]
+    def scores_of(slot, g, chunk, blocks, causal, first, last):
+        q = qs[g, :, chunk * 256 : (chunk + 1) * 256]
+        for i, (src, blk, _) in enumerate(blocks):
+            s_buf[slot, i * BLK : (i + 1) * BLK] = mm(kv[src, 2 * blk + g, 0:128], q)
+
+    def weights_of(slot, g, chunk, blocks, causal, first, last):
+        lanes = slice(chunk * 256, (chunk + 1) * 256)
         low = low_row[0:1, lanes]
-        scores = []
-        for slot, blk, back in blocks:
-            s = lax.dot_general(
-                kv[slot, 2 * blk + g, 0:128], q, NT, preferred_element_type=jnp.float32
-            )
+        parts = []
+        for i, (_, blk, back) in enumerate(blocks):
             k_pos = ((here - back) * 2 + blk) * BLK + lax.broadcasted_iota(
                 jnp.int32, (BLK, 256), 0
             )
             allowed = k_pos >= low
             if causal:
                 allowed = allowed & (k_pos <= pos_row[0:1, lanes])
-            scores.append(jnp.where(allowed, s * factor, NEG))
-        top = functools.reduce(jnp.maximum, [jnp.max(s, axis=0, keepdims=True) for s in scores])
+            parts.append(jnp.where(allowed, s_buf[slot, i * BLK : (i + 1) * BLK] * factor, NEG))
+        top = functools.reduce(jnp.maximum, [p.reshape(BLK // 8, 8, 256).max(axis=0) for p in parts])
+        top = jnp.max(top, axis=0, keepdims=True)
         if not first:
             old = m_s[g, 0:1, lanes]
             top = jnp.maximum(old, top)
             shrink = jnp.exp2(old - top)
-        parts = [jnp.exp2(s - top) for s in scores]
-        total = sum(jnp.sum(p.reshape(BLK // 8, 8, 256), axis=0) for p in parts)
-        weights = jnp.concatenate([p.astype(jnp.bfloat16) for p in parts], axis=0)
-        values = jnp.concatenate([kv[slot, 2 * blk + g, 128:256] for slot, blk, _ in blocks], axis=1)
-        mixed = mm(values, weights)
-        if not first:
-            total = total + l_s[g, :, lanes] * shrink
-            mixed = mixed + acc_s[g, :, lanes] * shrink
+            shrink_s[slot, 0:1] = shrink
         if not last:
             m_s[g, 0:1, lanes] = top
-            l_s[g, :, lanes] = total
+        total = None
+        for i, s in enumerate(parts):
+            p = jnp.exp2(s - top)
+            p_buf[slot, i * BLK : (i + 1) * BLK] = p.astype(jnp.bfloat16)
+            p = p.reshape(BLK // 8, 8, 256).sum(axis=0)
+            total = p if total is None else total + p
+        l_s[g, :, lanes] = total if first else total + l_s[g, :, lanes] * shrink
+
+    def mix_of(slot, g, chunk, blocks, causal, first, last):
+        lanes = slice(chunk * 256, (chunk + 1) * 256)
+        values = jnp.concatenate([kv[src, 2 * blk + g, 128:256] for src, blk, _ in blocks], axis=1)
+        mixed = mm(values, p_buf[slot, 0 : len(blocks) * BLK])
+        if not first:
+            mixed = mixed + acc_s[g, :, lanes] * shrink_s[slot, 0:1]
+        if not last:
             acc_s[g, :, lanes] = mixed
             return
-        mixed = mixed / jnp.sum(total, axis=0, keepdims=True)
-        blk, pair = chunk // 2, lax.rem(chunk, 2)
-        rows = pl.ds(pl.multiple_of(blk * BLK, BLK), BLK)
+        mixed = mixed / jnp.sum(l_s[g, :, lanes], axis=0, keepdims=True)
+        rows = slice(chunk // 2 * BLK, (chunk // 2 + 1) * BLK)
         for j in range(2):
-            cols = pl.ds(pl.multiple_of((g * 4 + pair * 2 + j) * HEAD, HEAD), HEAD)
-            out[rows, cols] = mixed[:, j * HEAD : (j + 1) * HEAD].T.astype(jnp.bfloat16)
-
-    def sweep(g, chunks, blocks, **how):
-        def step(chunk, _):
-            update(g, chunk, blocks, **how)
-            return 0
-
-        lax.fori_loop(chunks[0], chunks[1], step, 0)
-
-    for g in range(2):
-        sweep(g, (0, 2), [(OWN, 0, 0)], causal=True, first=True)
-        sweep(g, (2, 4), [(OWN, 0, 0), (OWN, 1, 0)], causal=True, first=True)
+            at = g * 4 + chunk % 2 * 2 + j
+            out[rows, at * HEAD : (at + 1) * HEAD] = (
+                mixed[:, j * HEAD : (j + 1) * HEAD].T.astype(jnp.bfloat16)
+            )
+
+    def run(tasks):
+        count = len(tasks)
+        for i in range(count + 2):
+            for stage, j in ((scores_of, i), (mix_of, i - 2), (weights_of, i - 1)):
+                if 0 <= j < count:
+                    stage(j % 3, *tasks[j])
+
+    def task(g, chunk, blocks, causal=False, first=False, last=False):
+        return g, chunk, blocks, causal, first, last
+
+    own = [(OWN, 0, 0), (OWN, 1, 0)]
+    run(
+        [
+            task(g, chunk, own[: 1 + chunk // 2], causal=True, first=True)
+            for g in range(2)
+            for chunk in range(4)
+        ]
+    )
 
     for step in (relay_first, relay_second, relay_third):
         for i in range(2):
             by_column(functools.partial(step, i))
 
-    for g in range(2):
-        all_of([(BACK1, g), (BACK1, 2 + g)])
-        sweep(g, (0, 4), [(BACK1, 0, 1), (BACK1, 1, 1)])
-    for g in range(2):
-        all_of([(BACK3, g), (BACK3, 2 + g), (BACK4, 2 + g)])
-        sweep(g, (0, 2), [(BACK4, 1, 4), (BACK3, 0, 3), (BACK3, 1, 3)])
-        sweep(g, (2, 4), [(BACK3, 1, 3)])
+    all_of([(BACK1, piece) for piece in range(4)])
+    back1 = [(BACK1, 0, 1), (BACK1, 1, 1)]
+    run([task(g, chunk, back1) for g in range(2) for chunk in range(4)])
+    all_of([(BACK3, piece) for piece in range(4)] + [(BACK4, b) for b in B])
+    back3 = [(BACK4, 1, 4), (BACK3, 0, 3), (BACK3, 1, 3)]
+    run([task(g, chunk, back3[chunk // 2 * 2 :]) for g in range(2) for chunk in range(4)])
+    back2 = [(BACK2, 0, 2), (BACK2, 1, 2)]
     for g in range(2):
         all_of([(BACK2, g), (BACK2, 2 + g)])
-        sweep(g, (0, 4), [(BACK2, 0, 2), (BACK2, 1, 2)], last=True)
+        run([task(g, chunk, back2, last=True) for chunk in range(4)])
 
     for swap in swaps:
         swap.wait_send()
 
     def finish(col):
-        for k in range(sends[col]):
-            copy(OWN, BACK1, 0, up, k).wait_send()
+        for kind in range(3):
+            for k in range(sends[col][kind]):
+                guarded(kind, lambda k=8 * kind + k: copy(OWN, BACK1, 0, up, k).wait_send())
 
     by_column(finish)
 
@@ -360,17 +407,20 @@
             pltpu.VMEM((2, half, k_cols), bf16),
             pltpu.VMEM((rows, 2 * k_cols), f32),
             pltpu.VMEM((rows, q_cols), f32),
-            pltpu.VMEM((groups, lanes, HEAD), bf16),
+            pltpu.VMEM((groups, HEAD, lanes), bf16),
             pltpu.VMEM((8, 4, 2 * BLK, HEAD), bf16),
             pltpu.VMEM((8, lanes), jnp.int32),
             pltpu.VMEM((8, lanes), jnp.int32),
             pltpu.VMEM((groups, 8, lanes), f32),
             pltpu.VMEM((groups, 8, lanes), f32),
             pltpu.VMEM((groups, HEAD, lanes), f32),
+            pltpu.VMEM((3, 3 * BLK, 256), f32),
+            pltpu.VMEM((3, 3 * BLK, 256), bf16),
+            pltpu.VMEM((3, 8, 256), f32),
             dma((7,)),
             dma((2,)),
             dma((2,)),
-            dma((20,)),
+            dma((24,)),
             dma((8, 4)),
         ],
         compiler_params=pltpu.CompilerParams(

time: 37.9 us -> 28.8 us (0.76)
  the two profiles are of different devices: /device:TPU:0 before, /device:TPU:24 now
where the time goes in v2:
time: 28.8 us; the launch traced here: 28.7 us
  Pallas kernels  26.8 us (93%)
  local copies, waits for them, and re-layouts  1.87 us (6%)
    pallas_call x1, Pallas kernels, local(): pl.pallas_call(functools.partial(kernel, shards), out_shape=jax.ShapeDtyp...  26.8 us
    unnamed x1, local copies, waits for them, and re-layouts  1.87 us

profile of v2, /device:TPU:24, one launch (start us, length us, event | category | flops | bytes accessed | tf_op | source)
XLA Modules:
  0.0 28.7 jit_solution(7590385784040368585)
XLA Ops:
  0.0 26.8 %attention.1 = bf16[256,1024]{1,0:T(8,128)(2,1)} custom-call(bf16[256,2048]{1,0:T(8,128)(2,1)} %hid.1, s32[128]{0:T(128)} %owner.1, s32[32]{0:T(128)} %lengths.1, bf16[4096,1024]{1,0:T(8,128)(2,1)} %w_q.1, bf16[4096,256]{1,0:T(8,128)(2,1)} %w_k.1, bf16[4096,256]{1,0:T(8,128)(2,1)} %w_v.1), custom_call_target="tpu_custom_call" | custom-call | flops 6442450944 | bytes 16777216 | tf_op jit(solution)/shard_map/attention/pallas_call | solution.py:397
  26.8 1.9 %copy.8 = bf16[256,1024]{1,0:T(8,128)(2,1)} copy(bf16[256,1024]{1,0:T(8,128)(2,1)} %attention.1) | data formatting | bytes 1048576

commit v3 on v2

--- a/solution.py
+++ b/solution.py
@@ -19,12 +19,14 @@
 def kernel(
     shards,
     hid,
-    owner,
-    lengths,
+    owner_hbm,
+    lengths_hbm,
     w_q,
     w_k,
     w_v,
     out,
+    owner,
+    lengths,
     h_own,
     h_oth,
     wq,
@@ -74,7 +76,11 @@
                 w_q.at[pl.ds(first, half)], wq.at[part], load_sem.at[len(loads)]
             )
         )
-    for load in loads:
+    tables = [
+        pltpu.make_async_copy(owner_hbm, owner, load_sem.at[7]),
+        pltpu.make_async_copy(lengths_hbm, lengths, load_sem.at[8]),
+    ]
+    for load in tables + loads:
         load.start()
     load_h, load_k0, load_v0, load_k1, load_v1, load_q0, load_q1 = loads
 
@@ -103,6 +109,8 @@
         )
         swaps[-1].start()
 
+    for table in tables:
+        table.wait()
     first_block = 2 * here - 8
     lane = lax.broadcasted_iota(jnp.int32, (8, BLK), 1)
     for blk in range(2):
@@ -392,14 +400,15 @@
     lanes = rows * q_cols // k_cols
     dma = pltpu.SemaphoreType.DMA
     any_spec = pl.BlockSpec(memory_space=pl.ANY)
-    smem_spec = pl.BlockSpec(memory_space=pltpu.SMEM)
     macs = rows * 2 * half * (q_cols + 2 * k_cols)
     return pl.pallas_call(
         functools.partial(kernel, shards),
-        out_shape=jax.ShapeDtypeStruct((rows, q_cols), bf16),
-        in_specs=[any_spec, smem_spec, smem_spec, any_spec, any_spec, any_spec],
+        out_shape=pltpu.VMEM((rows, q_cols), bf16),
+        in_specs=[any_spec] * 6,
         out_specs=pl.BlockSpec(memory_space=pltpu.VMEM),
         scratch_shapes=[
+            pltpu.SMEM(block_owner.shape, jnp.int32),
+            pltpu.SMEM(doc_lengths.shape, jnp.int32),
             pltpu.VMEM((rows, half), bf16),
             pltpu.VMEM((rows, half), bf16),
             pltpu.VMEM((2, half, q_cols), bf16),
@@ -417,7 +426,7 @@
             pltpu.VMEM((3, 3 * BLK, 256), f32),
             pltpu.VMEM((3, 3 * BLK, 256), bf16),
             pltpu.VMEM((3, 8, 256), f32),
-            dma((7,)),
+            dma((9,)),
             dma((2,)),
             dma((2,)),
             dma((24,)),

time: 28.8 us -> 26.2 us (0.910)
  Pallas kernels: 26.8 us -> 25.3 us
  local copies, waits for them, and re-layouts: 1.87 us -> 0.8 us
    pallas_call x1, Pallas kernels: 26.8 us -> 25.3 us  [local(): pl.pallas_call(functools.partial(kernel, shards), out_shape=pltpu.VMEM((r...]
    unnamed x1, local copies, waits for them, and re-layouts: 1.87 us -> 0.8 us
where the time goes in v3:
time: 26.2 us
  Pallas kernels  25.3 us (97%)
  local copies, waits for them, and re-layouts  0.8 us (3%)
    pallas_call x1, Pallas kernels, local(): pl.pallas_call(functools.partial(kernel, shards), out_shape=pltpu.VMEM((r...  25.3 us
    unnamed x1, local copies, waits for them, and re-layouts  0.8 us

profile of v3, /device:TPU:24, one launch (start us, length us, event | category | flops | bytes accessed | tf_op | source)
XLA Modules:
  0.0 26.2 jit_solution(11714715119082048990)
XLA Ops:
  0.0 25.3 %attention.1 = bf16[256,1024]{1,0:T(8,128)(2,1)S(1)} custom-call(bf16[256,2048]{1,0:T(8,128)(2,1)} %hid.1, s32[128]{0:T(128)} %owner_hbm.1, s32[32]{0:T(128)} %lengths_hbm.1, bf16[4096,1024]{1,0:T(8,128)(2,1)} %w_q.1, bf16[4096,256]{1,0:T(8,128)(2,1)} %w_k.1, bf16[4096,256]{1,0:T(8,128)(2,1)} %w_v.1), custom_call_target="tpu_custom_call" | custom-call | flops 6442450944 | bytes 16777216 | tf_op jit(solution)/shard_map/attention/pallas_call | solution.py:404
  25.4 0.8 %copy.8 = bf16[256,1024]{1,0:T(8,128)(2,1)} copy(bf16[256,1024]{1,0:T(8,128)(2,1)S(1)} %attention.1) | data formatting | bytes 1048576

commit v4 on v3

--- a/solution.py
+++ b/solution.py
@@ -263,7 +263,7 @@
         q_sum[:, cols] = mm(h_own[...], wq[0, :, cols])
         return 0
 
-    lax.fori_loop(0, 4, q_own, 0)
+    lax.fori_loop(0, 2, q_own, 0)
 
     for blk in range(2):
         swaps[blk].wait_recv()
@@ -279,6 +279,7 @@
             kv[OWN, 2 * blk + g, 128:256] = values[:, cols].T.astype(jnp.bfloat16)
         by_column(send_first if blk == 0 else send_second)
 
+    lax.fori_loop(2, 4, q_own, 0)
     load_q1.wait()
 
     def q_oth(n, _):
@@ -357,6 +358,8 @@
         return g, chunk, blocks, causal, first, last
 
     own = [(OWN, 0, 0), (OWN, 1, 0)]
+    for i in range(2):
+        by_column(functools.partial(relay_first, i))
     run(
         [
             task(g, chunk, own[: 1 + chunk // 2], causal=True, first=True)
@@ -365,9 +368,9 @@
         ]
     )
 
-    for step in (relay_first, relay_second, relay_third):
-        for i in range(2):
-            by_column(functools.partial(step, i))
+    for i in range(2):
+        by_column(functools.partial(relay_second, i))
+        by_column(functools.partial(relay_third, i))
 
     all_of([(BACK1, piece) for piece in range(4)])
     back1 = [(BACK1, 0, 1), (BACK1, 1, 1)]

time: 26.2 us -> 25.5 us (0.973)
  Pallas kernels: 25.3 us -> 24.6 us
    pallas_call x1, Pallas kernels: 25.3 us -> 24.6 us  [local(): pl.pallas_call(functools.partial(kernel, shards), out_shape=pltpu.VMEM((r...]
where the time goes in v4:
time: 25.5 us; the launch traced here: 25.4 us
  Pallas kernels  24.6 us (96%)
  local copies, waits for them, and re-layouts  0.8 us (3%)
    pallas_call x1, Pallas kernels, local(): pl.pallas_call(functools.partial(kernel, shards), out_shape=pltpu.VMEM((r...  24.6 us
    unnamed x1, local copies, waits for them, and re-layouts  0.8 us

profile of v4, /device:TPU:24, one launch (start us, length us, event | category | flops | bytes accessed | tf_op | source)
XLA Modules:
  0.0 25.4 jit_solution(527707303499849663)
XLA Ops:
  0.0 24.6 %attention.1 = bf16[256,1024]{1,0:T(8,128)(2,1)S(1)} custom-call(bf16[256,2048]{1,0:T(8,128)(2,1)} %hid.1, s32[128]{0:T(128)} %owner_hbm.1, s32[32]{0:T(128)} %lengths_hbm.1, bf16[4096,1024]{1,0:T(8,128)(2,1)} %w_q.1, bf16[4096,256]{1,0:T(8,128)(2,1)} %w_k.1, bf16[4096,256]{1,0:T(8,128)(2,1)} %w_v.1), custom_call_target="tpu_custom_call" | custom-call | flops 6442450944 | bytes 16777216 | tf_op jit(solution)/shard_map/attention/pallas_call | solution.py:407
  24.7 0.8 %copy.8 = bf16[256,1024]{1,0:T(8,128)(2,1)} copy(bf16[256,1024]{1,0:T(8,128)(2,1)S(1)} %attention.1) | data formatting | bytes 1048576

commit v5 on v4

--- a/solution.py
+++ b/solution.py
@@ -372,12 +372,12 @@
         by_column(functools.partial(relay_second, i))
         by_column(functools.partial(relay_third, i))
 
+    all_of([(BACK3, piece) for piece in range(4)] + [(BACK4, b) for b in B])
+    back3 = [(BACK4, 1, 4), (BACK3, 0, 3), (BACK3, 1, 3)]
+    run([task(g, chunk, back3[chunk // 2 * 2 :]) for g in range(2) for chunk in range(4)])
     all_of([(BACK1, piece) for piece in range(4)])
     back1 = [(BACK1, 0, 1), (BACK1, 1, 1)]
     run([task(g, chunk, back1) for g in range(2) for chunk in range(4)])
-    all_of([(BACK3, piece) for piece in range(4)] + [(BACK4, b) for b in B])
-    back3 = [(BACK4, 1, 4), (BACK3, 0, 3), (BACK3, 1, 3)]
-    run([task(g, chunk, back3[chunk // 2 * 2 :]) for g in range(2) for chunk in range(4)])
     back2 = [(BACK2, 0, 2), (BACK2, 1, 2)]
     for g in range(2):
         all_of([(BACK2, g), (BACK2, 2 + g)])

time: 25.5 us -> 24.9 us (0.976)
  Pallas kernels: 24.6 us -> 24 us
    pallas_call x1, Pallas kernels: 24.6 us -> 24 us  [local(): pl.pallas_call(functools.partial(kernel, shards), out_shape=pltpu.VMEM((r...]
where the time goes in v5:
time: 24.9 us; the launch traced here: 24.8 us
  Pallas kernels  24 us (96%)
  local copies, waits for them, and re-layouts  0.8 us (3%)
    pallas_call x1, Pallas kernels, local(): pl.pallas_call(functools.partial(kernel, shards), out_shape=pltpu.VMEM((r...  24 us
    unnamed x1, local copies, waits for them, and re-layouts  0.8 us

profile of v5, /device:TPU:24, one launch (start us, length us, event | category | flops | bytes accessed | tf_op | source)
XLA Modules:
  0.0 24.8 jit_solution(1085564283159421678)
XLA Ops:
  0.0 24.0 %attention.1 = bf16[256,1024]{1,0:T(8,128)(2,1)S(1)} custom-call(bf16[256,2048]{1,0:T(8,128)(2,1)} %hid.1, s32[128]{0:T(128)} %owner_hbm.1, s32[32]{0:T(128)} %lengths_hbm.1, bf16[4096,1024]{1,0:T(8,128)(2,1)} %w_q.1, bf16[4096,256]{1,0:T(8,128)(2,1)} %w_k.1, bf16[4096,256]{1,0:T(8,128)(2,1)} %w_v.1), custom_call_target="tpu_custom_call" | custom-call | flops 6442450944 | bytes 16777216 | tf_op jit(solution)/shard_map/attention/pallas_call | solution.py:407
  24.0 0.8 %copy.8 = bf16[256,1024]{1,0:T(8,128)(2,1)} copy(bf16[256,1024]{1,0:T(8,128)(2,1)S(1)} %attention.1) | data formatting | bytes 1048576

commit v6 on v5

--- a/solution.py
+++ b/solution.py
@@ -62,6 +62,14 @@
     mine = pl.multiple_of(head * half, half)
     other = pl.multiple_of((1 - head) * half, half)
 
+    @pl.when(here < 4)
+    def _():
+        for slot in (BACK1, BACK3, BACK2, BACK4):
+            kv[slot] = jnp.zeros(kv.shape[1:], kv.dtype)
+
+    barrier = pltpu.get_barrier_semaphore()
+    for peer in ((here, 1 - head), (up, head), (down, head), (row_prev, head)):
+        pl.semaphore_signal(barrier, inc=1, device_id=peer, device_id_type=MESH)
     loads = [pltpu.make_async_copy(hid, h_own, load_sem.at[0])]
     for part, first in ((0, mine), (1, other)):
         for src, dst in ((w_k, wk), (w_v, wv)):
@@ -84,14 +92,6 @@
         load.start()
     load_h, load_k0, load_v0, load_k1, load_v1, load_q0, load_q1 = loads
 
-    @pl.when(here < 4)
-    def _():
-        for slot in (BACK1, BACK3, BACK2, BACK4):
-            kv[slot] = jnp.zeros(kv.shape[1:], kv.dtype)
-
-    barrier = pltpu.get_barrier_semaphore()
-    for peer in ((here, 1 - head), (up, head), (down, head), (row_prev, head)):
-        pl.semaphore_signal(barrier, inc=1, device_id=peer, device_id_type=MESH)
     pl.semaphore_wait(barrier, 4)
 
     swaps = []
@@ -256,14 +256,6 @@
     kv_sum[:, 0:256] = mm(h_own[...], wk[0])
     load_v0.wait()
     kv_sum[:, 256:512] = mm(h_own[...], wv[0])
-    load_q0.wait()
-
-    def q_own(n, _):
-        cols = pl.ds(pl.multiple_of(n * 256, 256), 256)
-        q_sum[:, cols] = mm(h_own[...], wq[0, :, cols])
-        return 0
-
-    lax.fori_loop(0, 2, q_own, 0)
 
     for blk in range(2):
         swaps[blk].wait_recv()
@@ -279,7 +271,14 @@
             kv[OWN, 2 * blk + g, 128:256] = values[:, cols].T.astype(jnp.bfloat16)
         by_column(send_first if blk == 0 else send_second)
 
-    lax.fori_loop(2, 4, q_own, 0)
+    load_q0.wait()
+
+    def q_own(n, _):
+        cols = pl.ds(pl.multiple_of(n * 256, 256), 256)
+        q_sum[:, cols] = mm(h_own[...], wq[0, :, cols])
+        return 0
+
+    lax.fori_loop(0, 4, q_own, 0)
     load_q1.wait()
 
     def q_oth(n, _):
@@ -292,7 +291,7 @@
                 qs[g, :, pl.ds(first, BLK)] = q[blk * BLK : (blk + 1) * BLK, j * HEAD : (j + 1) * HEAD].T
         return 0
 
-    lax.fori_loop(0, 4, q_oth, 0)
+    lax.fori_loop(0, 1, q_oth, 0)
 
     factor = math.log2(math.e) / math.sqrt(HEAD)
 
@@ -358,17 +357,11 @@
         return g, chunk, blocks, causal, first, last
 
     own = [(OWN, 0, 0), (OWN, 1, 0)]
+    by_column(functools.partial(relay_first, 0))
+    lax.fori_loop(1, 4, q_oth, 0)
+    by_column(functools.partial(relay_first, 1))
     for i in range(2):
-        by_column(functools.partial(relay_first, i))
-    run(
-        [
-            task(g, chunk, own[: 1 + chunk // 2], causal=True, first=True)
-            for g in range(2)
-            for chunk in range(4)
-        ]
-    )
-
-    for i in range(2):
+        run([task(i, chunk, own[: 1 + chunk // 2], causal=True, first=True) for chunk in range(4)])
         by_column(functools.partial(relay_second, i))
         by_column(functools.partial(relay_third, i))
 

time: 24.9 us -> 24 us (0.964)
  Pallas kernels: 24 us -> 22.9 us
    pallas_call x1, Pallas kernels: 24 us -> 22.9 us  [local(): pl.pallas_call(functools.partial(kernel, shards), out_shape=pltpu.VMEM((r...]
where the time goes in v6:
time: 24 us; the launch traced here: 23.8 us
  Pallas kernels  22.9 us (95%)
  local copies, waits for them, and re-layouts  0.8 us (3%)
    pallas_call x1, Pallas kernels, local(): pl.pallas_call(functools.partial(kernel, shards), out_shape=pltpu.VMEM((r...  22.9 us
    unnamed x1, local copies, waits for them, and re-layouts  0.8 us

profile of v6, /device:TPU:24, one launch (start us, length us, event | category | flops | bytes accessed | tf_op | source)
XLA Modules:
  0.0 23.8 jit_solution(9103220317654228139)
XLA Ops:
  0.0 22.9 %attention.1 = bf16[256,1024]{1,0:T(8,128)(2,1)S(1)} custom-call(bf16[256,2048]{1,0:T(8,128)(2,1)} %hid.1, s32[128]{0:T(128)} %owner_hbm.1, s32[32]{0:T(128)} %lengths_hbm.1, bf16[4096,1024]{1,0:T(8,128)(2,1)} %w_q.1, bf16[4096,256]{1,0:T(8,128)(2,1)} %w_k.1, bf16[4096,256]{1,0:T(8,128)(2,1)} %w_v.1), custom_call_target="tpu_custom_call" | custom-call | flops 6442450944 | bytes 16777216 | tf_op jit(solution)/shard_map/attention/pallas_call | solution.py:400
  23.0 0.8 %copy.8 = bf16[256,1024]{1,0:T(8,128)(2,1)} copy(bf16[256,1024]{1,0:T(8,128)(2,1)S(1)} %attention.1) | data formatting | bytes 1048576

commit v7 on v6

--- a/solution.py
+++ b/solution.py
@@ -88,7 +88,7 @@
         pltpu.make_async_copy(owner_hbm, owner, load_sem.at[7]),
         pltpu.make_async_copy(lengths_hbm, lengths, load_sem.at[8]),
     ]
-    for load in tables + loads:
+    for load in tables + loads[:5]:
         load.start()
     load_h, load_k0, load_v0, load_k1, load_v1, load_q0, load_q1 = loads
 
@@ -108,6 +108,8 @@
             )
         )
         swaps[-1].start()
+    load_q0.start()
+    load_q1.start()
 
     for table in tables:
         table.wait()

time: 24 us -> 24 us (level)
  no operation moved by 1% of the time
where the time goes in v7:
time: 24 us; the launch traced here: 23.8 us
  Pallas kernels  22.9 us (95%)
  local copies, waits for them, and re-layouts  0.8 us (3%)
    pallas_call x1, Pallas kernels, local(): pl.pallas_call(functools.partial(kernel, shards), out_shape=pltpu.VMEM((r...  22.9 us
    unnamed x1, local copies, waits for them, and re-layouts  0.8 us

profile of v7, /device:TPU:24, one launch (start us, length us, event | category | flops | bytes accessed | tf_op | source)
XLA Modules:
  0.0 23.8 jit_solution(174061651729285006)
XLA Ops:
  0.0 22.9 %attention.1 = bf16[256,1024]{1,0:T(8,128)(2,1)S(1)} custom-call(bf16[256,2048]{1,0:T(8,128)(2,1)} %hid.1, s32[128]{0:T(128)} %owner_hbm.1, s32[32]{0:T(128)} %lengths_hbm.1, bf16[4096,1024]{1,0:T(8,128)(2,1)} %w_q.1, bf16[4096,256]{1,0:T(8,128)(2,1)} %w_k.1, bf16[4096,256]{1,0:T(8,128)(2,1)} %w_v.1), custom_call_target="tpu_custom_call" | custom-call | flops 6442450944 | bytes 16777216 | tf_op jit(solution)/shard_map/attention/pallas_call | solution.py:402
  23.0 0.8 %copy.8 = bf16[256,1024]{1,0:T(8,128)(2,1)} copy(bf16[256,1024]{1,0:T(8,128)(2,1)S(1)} %attention.1) | data formatting | bytes 1048576
